TPU v7x, 32 devices: a whole 2x2x4 slice. The times are simulated.
32 devices in a mesh: ctx: 16 (over z, x, core), tp: 2 (over y).
Axes of the slice: x: 2, y: 2, z: 4, core: 2. Of those that a mesh axis runs over, the one named last changes fastest.
Arguments:
- ctx_queries: bfloat16 [4096, 4096], P('ctx', 'tp'), may hold values from -5 to 5
- ctx_keys: bfloat16 [4096, 1024], P('ctx', 'tp'), may hold values from -5 to 5
- ctx_values: bfloat16 [4096, 1024], P('ctx', 'tp'), may hold values from -18 to 18
- query_queries: bfloat16 [512, 4096], P(None, 'tp'), may hold values from -5 to 5
- query_keys: bfloat16 [512, 1024], P('ctx', 'tp'), may hold values from -5 to 5
- query_values: bfloat16 [512, 1024], P('ctx', 'tp'), may hold values from -18 to 18
- out_weight: bfloat16 [4096, 4096], P('tp', 'ctx'), may hold values from -0.09375 to 0.09375
Outputs:
- ctx_out: bfloat16 [4096, 4096], P('ctx', 'tp')
- query_out: bfloat16 [512, 4096], P('tp', 'ctx')
All inputs are finite; a program needn't handle non-finite values.
Results may differ from a plain program's by a relative error of at most 0.0049.
Values may be sent and summed in bfloat16 or wider, within the bound.
A program may use at most 192 MiB of HBM per device.

v0:
```python
import math

import jax
import jax.numpy as jnp
from jax import lax
from jax.sharding import PartitionSpec as P

HD = 128
QL = 512


def spread(block, axis, source):
    block = jnp.where(lax.axis_index(axis) == source, block, jnp.zeros_like(block))
    return lax.psum(block, axis)


def attend_part(query_part, key_part, value_part, visible):
    scale = HD ** (-0.5)
    scores = (
        jnp.einsum("tkgd,skd->tkgs", query_part, key_part, preferred_element_type=jnp.float32)
        * scale
    )
    scores = jnp.where(visible[:, None, None, :], scores, -jnp.inf)
    top = jnp.max(scores, axis=-1)
    weights = jnp.exp(scores - top[..., None])
    total = jnp.sum(weights, axis=-1)
    probs = weights.astype(jnp.bfloat16)
    summed = jnp.einsum("tkgs,skd->tkgd", probs, value_part, preferred_element_type=jnp.float32)
    return (top, total, summed)


def body(ctx_queries, ctx_keys, ctx_values, query_queries, query_keys, query_values, out_weight):
    block_len = ctx_queries.shape[0]
    kv_local = ctx_keys.shape[1] // HD
    group = ctx_queries.shape[1] // ctx_keys.shape[1]
    index = lax.axis_index("ctx")
    anchor_keys, anchor_values = (spread(ctx_keys, "ctx", 0), spread(ctx_values, "ctx", 0))
    key_rows = jnp.concatenate([anchor_keys, ctx_keys], 0).reshape(2 * block_len, kv_local, HD)
    value_rows = jnp.concatenate([anchor_values, ctx_values], 0).reshape(
        2 * block_len, kv_local, HD
    )
    query_grid = ctx_queries.reshape(block_len, kv_local, group, HD)
    width = math.gcd(block_len, 128)

    def context_piece(start):
        rows = lax.dynamic_slice_in_dim(query_grid, start, width, 0)
        position = start + jnp.arange(width)
        own_seen = position[:, None] >= jnp.arange(block_len)[None, :]
        anchor_seen = jnp.broadcast_to(index > 0, (width, block_len))
        visible = jnp.concatenate([anchor_seen, own_seen], 1)
        top, total, summed = attend_part(rows, key_rows, value_rows, visible)
        return (summed / total[..., None]).astype(jnp.bfloat16).reshape(width, -1)

    ctx_starts = jnp.arange(block_len // width) * width
    ctx_out = lax.map(context_piece, ctx_starts).reshape(block_len, -1)
    share = query_keys.shape[0]
    own_keys = jnp.concatenate([ctx_keys, query_keys], 0).reshape(block_len + share, kv_local, HD)
    own_values = jnp.concatenate([ctx_values, query_values], 0).reshape(
        block_len + share, kv_local, HD
    )
    asked = query_queries.reshape(QL, kv_local, group, HD)
    key_pos = index * share + jnp.arange(share)
    query_width = math.gcd(QL, 128)

    def query_piece(start):
        rows = lax.dynamic_slice_in_dim(asked, start, query_width, 0)
        position = start + jnp.arange(query_width)
        visible = jnp.concatenate(
            [jnp.ones((query_width, block_len), dtype=bool), position[:, None] >= key_pos[None, :]],
            1,
        )
        return attend_part(rows, own_keys, own_values, visible)

    query_starts = jnp.arange(QL // query_width) * query_width
    tops, totals, sums = lax.map(query_piece, query_starts)
    local_top = tops.reshape(QL, kv_local, group)
    local_total = totals.reshape(QL, kv_local, group)
    local_sum = sums.reshape(QL, kv_local, group, HD)
    highest = lax.pmax(local_top, "ctx")
    factor = jnp.exp(local_top - highest)
    full_total, full_sum = lax.psum((local_total * factor, local_sum * factor[..., None]), "ctx")
    normed = (full_sum / full_total[..., None]).astype(jnp.bfloat16)
    attended = normed.reshape(QL, -1)
    rows = attended
    query_out = lax.psum_scatter(
        jnp.dot(rows, out_weight, preferred_element_type=jnp.float32),
        "tp",
        scatter_dimension=0,
        tiled=True,
    ).astype(jnp.bfloat16)
    return (ctx_out, query_out)


def solution(mesh):
    return jax.shard_map(
        body,
        mesh=mesh,
        in_specs=(
            P("ctx", "tp"),
            P("ctx", "tp"),
            P("ctx", "tp"),
            P(None, "tp"),
            P("ctx", "tp"),
            P("ctx", "tp"),
            P("tp", "ctx"),
        ),
        out_specs=(P("ctx", "tp"), P("tp", "ctx")),
        check_vma=False,
    )
```

profile of v0, /device:TPU:0, one launch (start us, length us, event | category | flops | bytes accessed | tf_op | source)
XLA Modules:
  0.0 264.4 jit_solution(10015377416520179371)
XLA Ops:
  10.6 2.9 %copy.34 = bf16[512,2048]{0,1:T(8,128)(2,1)S(1)} copy(bf16[512,2048]{1,0:T(8,128)(2,1)} %param.14) | data formatting | bytes 4194304 | tf_op args[3]
  13.5 1.8 copy_bitcast_fusion
  15.4 34.0 %while.28 = (s32[]{:T(128)}, f32[4,128,4,4]{1,0,3,2:T(4,128)S(1)}, f32[4,128,4,4]{1,0,3,2:T(4,128)}, f32[4,128,4,4,128]{4,1,0,3,2:T(8,128)}, s32[4]{0:T(128)S(1)...) while((s32[]{:T(128)}, f32[4,128,4,4]{1,0,3,2:T(4,128)S(1)}, ...), condition=%wide.region_9.10_spmd.clone, body=%wide.region_6.9_spmd.clone.sunk | while | flops 308478112 | bytes 9463744 | solution.py:75
  19.1 2.8 %fusion.56 = f32[4,128,4,4,128]{4,1,0,3,2:T(8,128)} fusion(f32[4,128,4,4,128]{4,1,0,3,2:T(8,128)} %get-tuple-element.389, s32[]{:T(128)} %get-tuple-element.386, f32[4,128,4,288]{1,3,2,0:T(8,128)S(1)} %get-tuple-element.342, f32[128,4,4]{0,2,1:T(4,128)S(1)} %get-tuple-element.341, pred[128,288]{0,1:T(8,128)(4,1)S(1)} %concatenate.26, ...), kind=kOutput, calls=%fused_computation.31.clone.1 | convolution fusion | flops 153354240 | bytes 3748352 | tf_op jit(solution)/shard_map/while/body/eval_jaxpr/tkgs,skd->tkgd/dot_general | solution.py:28
  22.4 1.4 dynamic_update_slice.29
  27.7 2.8 %fusion.56 = f32[4,128,4,4,128]{4,1,0,3,2:T(8,128)} fusion(f32[4,128,4,4,128]{4,1,0,3,2:T(8,128)} %get-tuple-element.389, s32[]{:T(128)} %get-tuple-element.386, f32[4,128,4,288]{1,3,2,0:T(8,128)S(1)} %get-tuple-element.342, f32[128,4,4]{0,2,1:T(4,128)S(1)} %get-tuple-element.341, pred[128,288]{0,1:T(8,128)(4,1)S(1)} %concatenate.26, ...), kind=kOutput, calls=%fused_computation.31.clone.1 | convolution fusion | flops 153354240 | bytes 3748352 | tf_op jit(solution)/shard_map/while/body/eval_jaxpr/tkgs,skd->tkgd/dot_general | solution.py:28
  30.9 1.4 dynamic_update_slice.29
  36.2 2.8 %fusion.56 = f32[4,128,4,4,128]{4,1,0,3,2:T(8,128)} fusion(f32[4,128,4,4,128]{4,1,0,3,2:T(8,128)} %get-tuple-element.389, s32[]{:T(128)} %get-tuple-element.386, f32[4,128,4,288]{1,3,2,0:T(8,128)S(1)} %get-tuple-element.342, f32[128,4,4]{0,2,1:T(4,128)S(1)} %get-tuple-element.341, pred[128,288]{0,1:T(8,128)(4,1)S(1)} %concatenate.26, ...), kind=kOutput, calls=%fused_computation.31.clone.1 | convolution fusion | flops 153354240 | bytes 3748352 | tf_op jit(solution)/shard_map/while/body/eval_jaxpr/tkgs,skd->tkgd/dot_general | solution.py:28
  39.4 1.4 dynamic_update_slice.29
  44.7 2.8 %fusion.56 = f32[4,128,4,4,128]{4,1,0,3,2:T(8,128)} fusion(f32[4,128,4,4,128]{4,1,0,3,2:T(8,128)} %get-tuple-element.389, s32[]{:T(128)} %get-tuple-element.386, f32[4,128,4,288]{1,3,2,0:T(8,128)S(1)} %get-tuple-element.342, f32[128,4,4]{0,2,1:T(4,128)S(1)} %get-tuple-element.341, pred[128,288]{0,1:T(8,128)(4,1)S(1)} %concatenate.26, ...), kind=kOutput, calls=%fused_computation.31.clone.1 | convolution fusion | flops 153354240 | bytes 3748352 | tf_op jit(solution)/shard_map/while/body/eval_jaxpr/tkgs,skd->tkgd/dot_general | solution.py:28
  48.0 1.4 dynamic_update_slice.29
  49.5 63.0 %pmax.7 = f32[512,4,4]{0,2,1:T(4,128)S(1)} all-reduce(f32[512,4,4]{0,2,1:T(4,128)S(1)} %reshape.63), channel_id=1, replica_groups=mesh['ctx'=16,'tp'=2] {'ctx'}, use_global_device_ids=true, to_apply=%region_10.11 | all-reduce | flops 8192 | bytes 65536 | tf_op jit(solution)/shard_map/pmax | solution.py:79
  113.3 4.2 %bitcast_multiply_fusion = f32[512,4,4,128]{3,0,2,1:T(8,128)} fusion(f32[4,128,4,4,128]{4,1,0,3,2:T(8,128)} %get-tuple-element.135, f32[512,4,4]{0,2,1:T(4,128)S(1)} %bitcast.140), kind=kLoop, calls=%fused_computation.46 | loop fusion | flops 1048576 | bytes 8421376 | tf_op jit(solution)/shard_map/mul | solution.py:81
  118.7 1.4 copy.26
  120.0 59.3 %psum.31 = f32[512,4,4]{0,2,1:T(4,128)S(1)} all-reduce(f32[512,4,4]{0,2,1:T(4,128)S(1)} %bitcast.141), channel_id=1, replica_groups=mesh['ctx'=16,'tp'=2] {'ctx'}, use_global_device_ids=true, to_apply=%region_12.13 | all-reduce | flops 8192 | bytes 65536 | tf_op jit(solution)/shard_map/psum | solution.py:81
  181.6 45.1 %all-reduce.6.cloned.1.call-done = f32[512,4,4,128]{3,0,2,1:T(8,128)} async-done(((f32[512,4,4,128]{3,0,2,1:T(8,128)}), f32[512,4,4,128]{3,0,2,1:T(8,128)}) %all-reduce.6.cloned.1.call-update) | async-done | bytes 4194320 | tf_op jit(solution)/shard_map/psum | solution.py:81
  226.7 3.9 %divide_convert_fusion.1 = bf16[512,4,4,128]{3,0,2,1:T(8,128)(2,1)} fusion(f32[512,4,4,128]{3,0,2,1:T(8,128)} %all-reduce.6.cloned.1.call-done, f32[512,4,4]{0,2,1:T(4,128)S(1)} %psum.31), kind=kLoop, calls=%fused_computation.47 | loop fusion | flops 2097152 | bytes 6324224 | tf_op jit(solution)/shard_map/convert_element_type | solution.py:82
  230.6 4.1 %copy.41 = bf16[512,4,4,128]{0,3,2,1:T(8,128)(2,1)} copy(bf16[512,4,4,128]{3,0,2,1:T(8,128)(2,1)} %divide_convert_fusion.1) | data formatting | bytes 4194304 | tf_op jit(solution)/shard_map/convert_element_type | solution.py:82
  234.7 3.1 %fusion.40 = f32[512,256]{1,0:T(8,128)} fusion(bf16[512,2048]{0,1:T(8,128)(2,1)} %bitcast.134, bf16[2048,256]{1,0:T(8,128)(2,1)S(1)} %copy-done), kind=kOutput, calls=%fused_computation.60 | convolution fusion | flops 536870912 | bytes 3670016 | tf_op jit(solution)/shard_map/dot_general | solution.py:86
  237.8 18.4 %while.27 = (s32[]{:T(128)}, bf16[2,128,2048]{2,1,0:T(8,128)(2,1)}, s32[2]{0:T(128)S(1)}, pred[]{:T(512)}, bf16[256,4,4,128]{0,3,2,1:T(8,128)(2,1)}, /*index=5*/...) while((s32[]{:T(128)}, bf16[2,128,2048]{2,1,0:T(8,128)(2,1)}, ...), condition=%wide.region_5.6_spmd, body=%wide.region_2.5_spmd.sunk | while | flops 548958336 | bytes 17147548 | solution.py:55
  241.1 2.5 bitcast_reduce_fusion.4
  243.6 1.3 fusion.52
  250.4 2.3 bitcast_reduce_fusion.4
  256.3 1.6 convert_element_type.20
  (86 shorter events, 26.0 us)
Async XLA Ops:
  7.2 227.5 %copy-start = (bf16[2048,256]{1,0:T(8,128)(2,1)S(1)}, bf16[2048,256]{1,0:T(8,128)(2,1)}, u32[]{:S(2)}) copy-start(bf16[2048,256]{1,0:T(8,128)(2,1)} %param.17) | copy-start | bytes 3145732
  7.2 6.3 %copy-start.6 = (bf16[32,512]{1,0:T(8,128)(2,1)S(1)}, bf16[32,512]{1,0:T(8,128)(2,1)}, u32[]{:S(2)}) copy-start(bf16[32,512]{1,0:T(8,128)(2,1)} %param.15) | copy-start | bytes 98308
  7.2 6.3 %copy-start.7 = (bf16[32,512]{1,0:T(8,128)(2,1)S(1)}, bf16[32,512]{1,0:T(8,128)(2,1)}, u32[]{:S(2)}) copy-start(bf16[32,512]{1,0:T(8,128)(2,1)} %param.16) | copy-start | bytes 98308
  7.2 172.1 %all-reduce.8.cloned.1.call-start = ((), (), s32[]{:S(2)}) async-start(), calls=%async_computation.3 | async-start | bytes 1048576 | tf_op jit(solution)/shard_map/psum | solution.py:14
  8.4 2.2 copy-start.3
  9.6 1.0 copy-start.1
  10.5 216.2 %all-reduce.6.cloned.1.call-start = ((), (), s32[]{:S(2)}) async-start(), calls=%async_computation.1 | async-start | bytes 8388608 | tf_op jit(solution)/shard_map/psum | solution.py:81
  117.4 1.2 copy-start.5
  117.4 61.9 %copy-start.4 = (bf16[256,512]{0,1:T(8,128)(2,1)S(1)}, bf16[256,512]{0,1:T(8,128)(2,1)}, u32[]{:S(2)}) copy-start(bf16[256,512]{0,1:T(8,128)(2,1)} %copy-done.3) | copy-start | bytes 786436
  117.5 63.1 %copy-start.2 = (bf16[256,512]{0,1:T(8,128)(2,1)S(1)}, bf16[256,512]{0,1:T(8,128)(2,1)}, u32[]{:S(2)}) copy-start(bf16[256,512]{0,1:T(8,128)(2,1)} %copy-done.1) | copy-start | bytes 786436
  117.5 138.8 %reduce-scatter.2.cloned.1.call-start = ((), (), s32[]{:S(2)}) async-start(), calls=%async_computation.2 | async-start | bytes 786432 | tf_op jit(solution)/shard_map/reduce_scatter | solution.py:85
Sparse Core Ops, SparseCore 0:
  11.5 92.6 all-reduce.7
  117.6 109.0 all-reduce.5
  238.0 13.4 reduce-scatter.1
where the time goes:
time: 266 us; the launch traced here: 264 us
  blocking collectives  122 us (46%)
  waiting for transfers between devices  45.2 us (17%)
  local copies, waits for them, and re-layouts  24.7 us (9%)
  matrix products  23.8 us (9%)
  other arithmetic  23.1 us (9%)
  between operations  13.9 us (5%)
  loops' own time  11.3 us (4%)
    pmax x1, blocking collectives, body(): highest = lax.pmax(local_top, 'ctx')  63 us
    psum x1, blocking collectives, body(): lax.psum((local_total * factor, local_sum * factor[..., None]), 'ctx')  59.3 us
    psum x1, waiting for transfers between devices, body(): lax.psum((local_total * factor, local_sum * factor[..., None]), 'ctx')  45.1 us
    dot_general x6, matrix products, attend_part(): jnp.einsum('tkgs,skd->tkgd', probs, value_part, preferred_element_type=jn...  13.6 us
    unnamed x20, local copies, waits for them, and re-layouts  7.74 us
    another operation x1, loops' own time, body(): tops, totals, sums = lax.map(query_piece, query_starts)  7.46 us
    dot_general x6, matrix products, attend_part(): jnp.einsum('tkgd,skd->tkgs', query_part, key_part, preferred_element_type...  7.05 us
    dynamic_update_slice x8, local copies, waits for them, and re-layouts, body(): tops, totals, sums = lax.map(query_piece, query_starts)  5.86 us
  transfers between devices with their start and end apart: 3, of which 1 were waited for; matrix products, arithmetic and copies ran while one was open for 21% of the time, Pallas kernels for 0%

commit v1 on v0

v1 whole, which is shorter than its diff:
```python
import functools
import math

import jax
import jax.numpy as jnp
from jax import lax
from jax.experimental import pallas as pl
from jax.experimental.pallas import tpu as pltpu
from jax.sharding import PartitionSpec as P

HD = 128
MESH = pl.DeviceIdType.MESH
COEF = HD ** (-0.5) * math.log2(math.e)
F32 = jnp.float32
BF16 = jnp.bfloat16
NEG = float("-inf")


def kernel(dims, cq_h, ck_h, cv_h, qq_h, qk_h, qv_h, w_h, co_h, qo_h, cq, ck, cv, ak, av, qq, w, kb, vb, kqb, vqb,
           acc, top, osend, lsend, orecv, lrecv, att, ysend, yrecv, co, qo, loc_sem, kv_s, kv_r, an_s, an_r, an_u,
           an_rs, an_rr, rs_s, rs_r, ag_r, ag_u, ag_d, ag_rs, ag_cs, y_s, y_r):
    groups, members, tps, kv_local, group, block, share, query_len = dims
    flat = group * query_len
    chunk = flat // members
    tile = min(256, chunk)
    pieces = math.gcd(members, block // 16)
    piece = block // pieces
    me = lax.axis_index("ctx")
    my_tp = lax.axis_index("tp")
    g = lax.div(me, members)
    m = lax.rem(me, members)
    pair = m + 1 - 2 * lax.rem(m, 2)

    def lanes(index):
        return pl.ds(pl.multiple_of(index * HD, HD), HD)

    def local(src, dst, i):
        return pltpu.make_async_copy(src, dst, loc_sem.at[i])

    def remote(src, dst, send, recv, to, axis="ctx"):
        return pltpu.make_async_remote_copy(src_ref=src, dst_ref=dst, send_sem=send, recv_sem=recv,
                                            device_id={axis: to}, device_id_type=MESH)

    wide = pl.ds(pl.multiple_of(g * (group * HD), HD), group * HD)
    own_rows = pl.ds(pl.multiple_of(g * share, share), share)
    loads = [
        local(qq_h.at[:, wide], qq, 0),
        local(ck_h.at[:, lanes(g)], kb.at[g], 1),
        local(cv_h.at[:, lanes(g)], vb.at[g], 2),
        local(ck_h, ck, 3),
        local(cv_h, cv, 4),
        local(cq_h, cq, 5),
        local(w_h, w, 6),
        local(qk_h.at[:, lanes(g)], kqb.at[own_rows], 7),
        local(qv_h.at[:, lanes(g)], vqb.at[own_rows], 8),
    ]
    if kqb.shape[0] > groups * share:
        kqb[...] = jnp.zeros_like(kqb)
        vqb[...] = jnp.zeros_like(vqb)
    for load in loads:
        load.start()

    @pl.when(me == 0)
    def _():
        local(ck_h, ak, 9).start()
        local(cv_h, av, 10).start()

    barrier = pltpu.get_barrier_semaphore()

    def greet_group(i, carry):
        to = g * members + lax.rem(m + i, members)
        pl.semaphore_signal(barrier, inc=1, device_id={"ctx": to}, device_id_type=MESH)
        return carry

    lax.fori_loop(1, members, greet_group, 0)
    for d in range(1, groups):
        to = lax.rem(g + d, groups) * members + m
        pl.semaphore_signal(barrier, inc=1, device_id={"ctx": to}, device_id_type=MESH)
    for d in range(1, tps):
        pl.semaphore_signal(barrier, inc=1, device_id={"tp": lax.rem(my_tp + d, tps)}, device_id_type=MESH)
    pl.semaphore_wait(barrier, members - 1 + groups - 1 + tps - 1)

    def piece_rows(p):
        return pl.ds(pl.multiple_of(p * piece, piece), piece)

    @pl.when(me == 0)
    def _():
        local(ck_h, ak, 9).wait()
        local(cv_h, av, 10).wait()
        for p in range(1, pieces):
            for k, buf in enumerate((ak, av)):
                remote(buf.at[piece_rows(p)], buf.at[piece_rows(p)], an_s.at[p, k], an_r.at[k], p).start()

    def kv_copies(to_group, slot):
        to = to_group * members + m
        rows = pl.ds(pl.multiple_of(slot * share, share), share)
        return [
            remote(ck_h.at[:, lanes(to_group)], kb.at[slot], kv_s.at[to_group, 0], kv_r.at[slot, 0], to),
            remote(cv_h.at[:, lanes(to_group)], vb.at[slot], kv_s.at[to_group, 1], kv_r.at[slot, 1], to),
            remote(qk_h.at[:, lanes(to_group)], kqb.at[rows], kv_s.at[to_group, 2], kv_r.at[slot, 2], to),
            remote(qv_h.at[:, lanes(to_group)], vqb.at[rows], kv_s.at[to_group, 3], kv_r.at[slot, 3], to),
        ]

    for d in range(1, groups):
        for copy in kv_copies(lax.rem(g + d, groups), g):
            copy.start()

    def attend(first_row, first, slot, with_query):
        head = lax.div(first_row, query_len)
        row = lax.rem(first_row, query_len)
        q = qq[pl.ds(pl.multiple_of(row, tile), tile), lanes(head)]
        keys, values = kb[slot], vb[slot]
        if with_query:
            keys = jnp.concatenate([keys, kqb[...]], 0)
            values = jnp.concatenate([values, vqb[...]], 0)
        values = jnp.concatenate([values, jnp.ones_like(values)], 1)
        s = lax.dot_general(q, keys, (((1,), (1,)), ((), ())), preferred_element_type=F32) * COEF
        if with_query:
            col = lax.broadcasted_iota(jnp.int32, s.shape, 1) - block
            at = lax.broadcasted_iota(jnp.int32, s.shape, 0) + row
            source = lax.div(jnp.maximum(col, 0), share)
            position = (source * members + m) * share + lax.rem(jnp.maximum(col, 0), share)
            seen = (col < 0) | ((at >= position) & (col < groups * share))
            s = jnp.where(seen, s, NEG)
        rows = pl.ds(pl.multiple_of(first_row, tile), tile)
        high = jnp.max(s, axis=1, keepdims=True)
        if not first:
            before = top[rows, :]
            high = jnp.maximum(high, before[:, :1])
        p = jnp.exp2(s - high).astype(BF16)
        o = jnp.dot(p, values, preferred_element_type=F32)
        if not first:
            o = o + acc[rows, :] * jnp.exp2(before[:, :1] - high)
        acc[rows, :] = o
        top[rows, :] = jnp.broadcast_to(high, (tile, HD))

    def sweep(slot, first):
        def step(t, carry):
            attend(t * tile, first, slot, False)
            return carry

        lax.fori_loop(0, flat // tile, step, 0, unroll=2)

    for i in (0, 1, 2):
        loads[i].wait()
    if groups > 1:
        sweep(g, True)

    for i in (3, 4, 5, 6, 7, 8):
        loads[i].wait()
    not_root = me > 0
    has_piece = m < pieces

    @pl.when(has_piece)
    def _():
        mine = piece_rows(m)
        for k, buf in enumerate((ak, av)):
            @pl.when(not_root)
            def _():
                remote(buf.at[mine], buf.at[mine], an_u.at[k], an_r.at[k], me).wait_recv()

            @pl.when(g + 1 < groups)
            def _():
                remote(buf.at[mine], buf.at[mine], an_u.at[k], an_r.at[k], lax.rem(me + members, groups * members)).start()

        def spread(i, carry):
            other = lax.rem(m + i, members)

            @pl.when((g > 0) | (other > 0))
            def _():
                for k, buf in enumerate((ak, av)):
                    remote(buf.at[mine], buf.at[mine], an_rs.at[other, k], an_rr.at[m, k], g * members + other).start()
            return carry

        lax.fori_loop(1, members, spread, 0)

    @pl.when(not_root)
    def _():
        def gather(p, carry):
            @pl.when(p != m)
            def _():
                for k, buf in enumerate((ak, av)):
                    remote(buf.at[piece_rows(p)], buf.at[piece_rows(p)], an_u.at[k], an_rr.at[p, k], me).wait_recv()
            return carry

        lax.fori_loop(0, pieces, gather, 0)

    def context_head(h):
        kv = lanes(lax.div(h, group))
        q = cq[:, lanes(h)]
        keys = jnp.concatenate([ak[:, kv], ck[:, kv]], 0)
        values = jnp.concatenate([av[:, kv], cv[:, kv]], 0)
        values = jnp.concatenate([values, jnp.ones_like(values)], 1)
        s = lax.dot_general(q, keys, (((1,), (1,)), ((), ())), preferred_element_type=F32) * COEF
        col = lax.broadcasted_iota(jnp.int32, s.shape, 1) - block
        at = lax.broadcasted_iota(jnp.int32, s.shape, 0)
        s = jnp.where((col <= at) & ((col >= 0) | not_root), s, NEG)
        p = jnp.exp2(s - jnp.max(s, axis=1, keepdims=True)).astype(BF16)
        o = jnp.dot(p, values, preferred_element_type=F32)
        co[:, lanes(h)] = (o[:, :HD] / o[:, HD:]).astype(BF16)

    def context_step(h, carry):
        context_head(h)
        return carry

    lax.fori_loop(0, kv_local * group, context_step, 0, unroll=2)
    store_ctx = local(co, co_h, 11)
    store_ctx.start()

    for d in range(1, groups):
        slot = lax.rem(g + d, groups)
        for copy in kv_copies(slot, slot):
            copy.wait_recv()
        if d < groups - 1:
            sweep(slot, False)
    last = lax.rem(g + groups - 1, groups)

    def part(to):
        rows = pl.ds(pl.multiple_of(to * chunk, chunk), chunk)
        total = acc[rows, HD:]
        return acc[rows, :HD] / total, top[rows, :] + jnp.log2(total)

    def attend_chunk(to):
        for t in range(chunk // tile):
            attend(to * chunk + t * tile, groups == 1, last, True)

    def part_copies(to, slot):
        target = g * members + to
        return [
            remote(osend.at[to], orecv.at[slot], rs_s.at[to, 0], rs_r.at[slot, 0], target),
            remote(lsend.at[to], lrecv.at[slot], rs_s.at[to, 1], rs_r.at[slot, 1], target),
        ]

    def send_part(i, carry):
        to = lax.rem(m + i, members)
        attend_chunk(to)
        out, lse = part(to)
        osend[to] = out.astype(BF16)
        lsend[to] = jnp.transpose(lse)[:8, :]
        for copy in part_copies(to, m):
            copy.start()
        return carry

    lax.fori_loop(1, members, send_part, 0)
    attend_chunk(m)
    own, own_lse = part(m)

    def wait_part(i, carry):
        for copy in part_copies(lax.rem(m + i, members), lax.rem(m + i, members)):
            copy.wait_recv()
        return carry

    lax.fori_loop(1, members, wait_part, 0)

    def lse_of(i):
        row = lrecv[lax.rem(m + i, members)][:1, :]
        return jnp.transpose(jnp.broadcast_to(row, (HD, chunk)))

    highest = lax.fori_loop(1, members, lambda i, high: jnp.maximum(high, lse_of(i)), own_lse)
    own_weight = jnp.exp2(own_lse - highest)

    def combine(i, carry):
        total, summed = carry
        weight = jnp.exp2(lse_of(i) - highest)
        return total + weight, summed + weight * orecv[lax.rem(m + i, members)].astype(F32)

    total, summed = lax.fori_loop(1, members, combine, (own_weight, own_weight * own))

    def place(of_group, of_member):
        start = of_member * chunk
        row = pl.multiple_of(lax.rem(start, query_len), chunk)
        return att.at[pl.ds(row, chunk), lanes(of_group * group + lax.div(start, query_len))]

    place(g, m)[...] = (summed / total).astype(BF16)

    def gathered(of_group, of_member, send, to):
        where = place(of_group, of_member)
        return remote(where, where, send, ag_r.at[of_group, of_member], to)

    def to_pair(of_group, of_member):
        return gathered(of_group, of_member, ag_cs.at[of_group, of_member], g * members + pair)

    def have(of_group):
        def across(i, carry):
            other = lax.rem(m + 2 * i, members)
            gathered(of_group, m, ag_rs.at[of_group, other], g * members + other).start()
            return carry

        lax.fori_loop(1, members // 2, across, 0)
        to_pair(of_group, m).start()

    def forward(of_group):
        def step(i, carry):
            other = lax.rem(m + 2 * i, members)
            gathered(of_group, other, ag_cs.at[of_group, other], me).wait_recv()
            to_pair(of_group, other).start()
            return carry

        lax.fori_loop(1, members // 2, step, 0)

    up = lax.rem(me + members, groups * members)
    down = lax.rem(me + (groups - 1) * members, groups * members)

    def when_low(s, run):
        pl.when(g - s >= 0)(lambda: run(jnp.maximum(g - s, 0)))

    def when_high(s, run):
        pl.when(g + s < groups)(lambda: run(jnp.minimum(g + s, groups - 1)))

    def relay_up(s):
        @pl.when((g - s >= 0) & (g + 1 < groups))
        def _():
            c = jnp.maximum(g - s, 0)
            gathered(c, m, ag_u.at[c], up).start()

    def relay_down(s):
        @pl.when((g + s < groups) & (g > 0))
        def _():
            c = jnp.minimum(g + s, groups - 1)
            gathered(c, m, ag_d.at[c], down).start()

    def arrive(c):
        gathered(c, m, ag_u.at[c], me).wait_recv()

    relay_up(0)
    relay_down(0)
    have(g)
    for s in range(1, groups):
        when_low(s, arrive)
        relay_up(s)
        when_low(s, have)
        when_high(s, arrive)
        relay_down(s)
        when_high(s, have)
        if s == 1:
            forward(g)
        else:
            when_low(s - 1, forward)
            when_high(s - 1, forward)
    if groups == 1:
        forward(g)
    else:
        when_low(groups - 1, forward)
        when_high(groups - 1, forward)

    def from_pair(i, carry):
        for c in range(groups):
            gathered(c, lax.rem(pair + 2 * i, members), ag_u.at[c], me).wait_recv()
        return carry

    lax.fori_loop(0, members // 2, from_pair, 0)

    out_rows = query_len // tps

    def project(of_tp):
        rows = pl.ds(pl.multiple_of(of_tp * out_rows, out_rows), out_rows)
        return jnp.dot(att[rows, :], w[...], preferred_element_type=F32)

    def sum_copy(of_tp, slot):
        return remote(ysend.at[of_tp], yrecv.at[slot], y_s.at[of_tp], y_r.at[slot], of_tp, "tp")

    for d in range(1, tps):
        to = lax.rem(my_tp + d, tps)
        ysend[to] = project(to).astype(BF16)
        sum_copy(to, my_tp).start()
    result = project(my_tp)
    for d in range(1, tps):
        source = lax.rem(my_tp + d, tps)
        sum_copy(source, source).wait_recv()
        result = result + yrecv[source].astype(F32)
    qo[...] = result.astype(BF16)
    store_query = local(qo, qo_h, 12)
    store_query.start()

    @pl.when(me == 0)
    def _():
        for p in range(1, pieces):
            for k, buf in enumerate((ak, av)):
                remote(buf.at[piece_rows(p)], buf.at[piece_rows(p)], an_s.at[p, k], an_r.at[k], p).wait_send()

    @pl.when(has_piece)
    def _():
        mine = piece_rows(m)

        @pl.when(g + 1 < groups)
        def _():
            for k, buf in enumerate((ak, av)):
                remote(buf.at[mine], buf.at[mine], an_u.at[k], an_r.at[k], me).wait_send()

        def spread_done(i, carry):
            other = lax.rem(m + i, members)

            @pl.when((g > 0) | (other > 0))
            def _():
                for k, buf in enumerate((ak, av)):
                    remote(buf.at[mine], buf.at[mine], an_rs.at[other, k], an_rr.at[m, k], me).wait_send()
            return carry

        lax.fori_loop(1, members, spread_done, 0)

    for d in range(1, groups):
        for copy in kv_copies(lax.rem(g + d, groups), g):
            copy.wait_send()

    def part_done(i, carry):
        for copy in part_copies(lax.rem(m + i, members), m):
            copy.wait_send()
        return carry

    lax.fori_loop(1, members, part_done, 0)
    for s in range(groups):
        @pl.when((g - s >= 0) & (g + 1 < groups))
        def _():
            c = jnp.maximum(g - s, 0)
            gathered(c, m, ag_u.at[c], up).wait_send()

        @pl.when((g + s < groups) & (g > 0))
        def _():
            c = jnp.minimum(g + s, groups - 1)
            gathered(c, m, ag_d.at[c], down).wait_send()

    def pair_done(i, carry):
        other = lax.rem(m + 2 * i, members)
        for c in range(groups):
            to_pair(c, other).wait_send()
        return carry

    lax.fori_loop(0, members // 2, pair_done, 0)

    def across_done(i, carry):
        other = lax.rem(m + 2 * i, members)
        for c in range(groups):
            gathered(c, m, ag_rs.at[c, other], me).wait_send()
        return carry

    lax.fori_loop(1, members // 2, across_done, 0)
    for d in range(1, tps):
        sum_copy(lax.rem(my_tp + d, tps), my_tp).wait_send()
    store_ctx.wait()
    store_query.wait()


def body(n_ctx, tps, ctx_queries, ctx_keys, ctx_values, query_queries, query_keys, query_values, out_weight):
    block, heads_wide = ctx_queries.shape
    kv_wide = ctx_keys.shape[1]
    kv_local = kv_wide // HD
    group = heads_wide // kv_wide
    share = query_keys.shape[0]
    query_len = query_queries.shape[0]
    groups = kv_local
    members = n_ctx // groups
    flat = group * query_len
    chunk = flat // members
    pieces = math.gcd(members, block // 16)
    query_rows = -(-groups * share // 128) * 128
    out_cols = out_weight.shape[1]
    out_rows = query_len // tps
    dims = (groups, members, tps, kv_local, group, block, share, query_len)
    any_spec = pl.BlockSpec(memory_space=pl.ANY)
    dma = pltpu.SemaphoreType.DMA
    vmem = pltpu.VMEM
    return pl.pallas_call(
        functools.partial(kernel, dims),
        out_shape=(
            jax.ShapeDtypeStruct((block, heads_wide), BF16),
            jax.ShapeDtypeStruct((out_rows, out_cols), BF16),
        ),
        in_specs=[any_spec] * 7,
        out_specs=(any_spec, any_spec),
        scratch_shapes=[
            vmem((block, heads_wide), BF16),
            vmem((block, kv_wide), BF16),
            vmem((block, kv_wide), BF16),
            vmem((block, kv_wide), BF16),
            vmem((block, kv_wide), BF16),
            vmem((query_len, group * HD), BF16),
            vmem(out_weight.shape, BF16),
            vmem((groups, block, HD), BF16),
            vmem((groups, block, HD), BF16),
            vmem((query_rows, HD), BF16),
            vmem((query_rows, HD), BF16),
            vmem((flat, 2 * HD), F32),
            vmem((flat, HD), F32),
            vmem((members, chunk, HD), BF16),
            vmem((members, 8, chunk), F32),
            vmem((members, chunk, HD), BF16),
            vmem((members, 8, chunk), F32),
            vmem((query_len, heads_wide), BF16),
            vmem((tps, out_rows, out_cols), BF16),
            vmem((tps, out_rows, out_cols), BF16),
            vmem((block, heads_wide), BF16),
            vmem((out_rows, out_cols), BF16),
            dma((13,)),
            dma((groups, 4)),
            dma((groups, 4)),
            dma((pieces, 2)),
            dma((2,)),
            dma((2,)),
            dma((members, 2)),
            dma((pieces, 2)),
            dma((members, 2)),
            dma((members, 2)),
            dma((groups, members)),
            dma((groups,)),
            dma((groups,)),
            dma((groups, members)),
            dma((groups, members)),
            dma((tps,)),
            dma((tps,)),
        ],
        compiler_params=pltpu.CompilerParams(
            collective_id=0, has_side_effects=True, vmem_limit_bytes=48 * 1024 * 1024
        ),
        cost_estimate=pl.CostEstimate(flops=3_000_000_000, bytes_accessed=8_000_000, transcendentals=4_000_000),
        name="star_attention",
    )(ctx_queries, ctx_keys, ctx_values, query_queries, query_keys, query_values, out_weight)


def solution(mesh):
    return jax.shard_map(
        functools.partial(body, mesh.shape["ctx"], mesh.shape["tp"]),
        mesh=mesh,
        in_specs=(
            P("ctx", "tp"),
            P("ctx", "tp"),
            P("ctx", "tp"),
            P(None, "tp"),
            P("ctx", "tp"),
            P("ctx", "tp"),
            P("tp", "ctx"),
        ),
        out_specs=(P("ctx", "tp"), P("tp", "ctx")),
        check_vma=False,
    )
```

time: 266 us -> 88.5 us (0.33)
  blocking collectives: 122 us -> 0 us
  Pallas kernels: 0 us -> 78.3 us
  waiting for transfers between devices: 45.2 us -> 0 us
  matrix products: 23.8 us -> 0 us
  other arithmetic: 23.1 us -> 0 us
  local copies, waits for them, and re-layouts: 24.7 us -> 9.07 us
  between operations: 13.9 us -> 0.66 us
  loops' own time: 11.3 us -> 0 us
    pallas_call x0 -> x1, Pallas kernels: none -> 78.3 us  [body(): pl.pallas_call(functools.partial(kernel, dims), out_shape=(jax.ShapeDtype...]
    pmax x1 -> x0, blocking collectives: 63 us -> none  [body(): highest = lax.pmax(local_top, 'ctx')]
    psum x1 -> x0, blocking collectives: 59.3 us -> none  [body(): lax.psum((local_total * factor, local_sum * factor[..., None]), 'ctx')]
    psum x2 -> x0, waiting for transfers between devices: 45.1 us -> none  [the longest x1 45.1 us: body(): lax.psum((local_total * factor, local_sum * factor[..., None]), 'ctx')]
    dot_general x13 -> x0, matrix products: 23.8 us -> none  [the longest x6 13.6 us: attend_part(): jnp.einsum('tkgs,skd->tkgd', probs, value_part, preferred_element_type=jn...]
    another operation x2 -> x0, loops' own time: 11.3 us -> none  [the longest x1 7.46 us: body(): tops, totals, sums = lax.map(query_piece, query_starts)]
    dynamic_update_slice x12 -> x0, local copies, waits for them, and re-layouts: 7.95 us -> none  [the longest x8 5.86 us: body(): tops, totals, sums = lax.map(query_piece, query_starts)]
    convert_element_type x2 -> x0, other arithmetic: 5.47 us -> none  [the longest x1 3.85 us: body(): normed = (full_sum / full_total[..., None]).astype(jnp.bfloat16)]
  transfers between devices with their start and end apart: 3 -> 0, of which waited for: 1 -> 0; matrix products, arithmetic and copies ran while one was open for 21% -> 0% of each run, Pallas kernels for 0% -> 0%
where the time goes in v1:
time: 88.5 us; the launch traced here: 88 us
  Pallas kernels  78.3 us (88%)
  local copies, waits for them, and re-layouts  9.07 us (10%)
    pallas_call x1, Pallas kernels, body(): pl.pallas_call(functools.partial(kernel, dims), out_shape=(jax.ShapeDtype...  78.3 us
    unnamed x16, local copies, waits for them, and re-layouts  9.07 us

profile of v1, /device:TPU:0, one launch (start us, length us, event | category | flops | bytes accessed | tf_op | source)
XLA Modules:
  0.0 88.0 jit_solution(16487653769977631152)
XLA Ops:
  0.6 0.0 copy-start
  0.6 1.6 %copy-done = bf16[512,2048]{1,0:T(8,128)(2,1)S(1)} copy-done((bf16[512,2048]{1,0:T(8,128)(2,1)S(1)}, bf16[512,2048]{1,0:T(8,128)(2,1)}, u32[]{:S(2)}) %copy-start) | copy-done | bytes 2097176
  2.2 0.0 copy-start.1
  2.2 1.2 %copy-done.1 = bf16[256,2048]{1,0:T(8,128)(2,1)S(1)} copy-done((bf16[256,2048]{1,0:T(8,128)(2,1)S(1)}, bf16[256,2048]{1,0:T(8,128)(2,1)}, u32[]{:S(2)}) %copy-start.1) | copy-done | bytes 1048600
  3.4 0.0 copy-start.2
  3.5 1.2 %copy-done.2 = bf16[2048,256]{1,0:T(8,128)(2,1)S(1)} copy-done((bf16[2048,256]{1,0:T(8,128)(2,1)S(1)}, bf16[2048,256]{1,0:T(8,128)(2,1)}, u32[]{:S(2)}) %copy-start.2) | copy-done | bytes 1048600
  4.7 0.0 copy-start.3
  4.7 0.9 %copy-done.3 = bf16[256,512]{1,0:T(8,128)(2,1)S(1)} copy-done((bf16[256,512]{1,0:T(8,128)(2,1)S(1)}, bf16[256,512]{1,0:T(8,128)(2,1)}, u32[]{:S(2)}) %copy-start.3) | copy-done | bytes 262168
  5.6 0.0 copy-start.4
  5.6 0.9 %copy-done.4 = bf16[256,512]{1,0:T(8,128)(2,1)S(1)} copy-done((bf16[256,512]{1,0:T(8,128)(2,1)S(1)}, bf16[256,512]{1,0:T(8,128)(2,1)}, u32[]{:S(2)}) %copy-start.4) | copy-done | bytes 262168
  6.6 0.0 copy-start.5
  6.6 0.8 copy-done.5
  7.3 0.0 copy-start.6
  7.3 0.8 copy-done.6
  8.1 78.3 %star_attention.1 = (bf16[256,2048]{1,0:T(8,128)(2,1)S(1)}, bf16[256,256]{1,0:T(8,128)(2,1)S(1)}) custom-call(bf16[256,2048]{1,0:T(8,128)(2,1)S(1)} %copy-done.1, bf16[256,512]{1,0:T(8,128)(2,1)S(1)} %copy-done.3, bf16[256,512]{1,0:T(8,128)(2,1)S(1)} %copy-done.4, bf16[512,2048]{1,0:T(8,128)(2,1)S(1)} %copy-done, bf16[32,512]{1,0:T(8,128)(2,1)S(1)} %copy-done.5, ...), custom_call_target="tpu_custom_call" | custom-call | flops 3000000000 | bytes 8000000 | tf_op jit(solution)/shard_map/star_attention/pallas_call | solution.py:462
  86.4 1.0 %copy.11 = bf16[256,2048]{1,0:T(8,128)(2,1)} copy(bf16[256,2048]{1,0:T(8,128)(2,1)S(1)} %get-tuple-element.4) | data formatting | bytes 2097152
  87.4 0.7 copy.12
Async XLA Ops:
  0.6 1.6 %copy-start = (bf16[512,2048]{1,0:T(8,128)(2,1)S(1)}, bf16[512,2048]{1,0:T(8,128)(2,1)}, u32[]{:S(2)}) copy-start(bf16[512,2048]{1,0:T(8,128)(2,1)} %qq_h.1) | copy-start | bytes 6291460
  2.2 1.2 %copy-start.1 = (bf16[256,2048]{1,0:T(8,128)(2,1)S(1)}, bf16[256,2048]{1,0:T(8,128)(2,1)}, u32[]{:S(2)}) copy-start(bf16[256,2048]{1,0:T(8,128)(2,1)} %cq_h.1) | copy-start | bytes 3145732
  3.4 1.2 %copy-start.2 = (bf16[2048,256]{1,0:T(8,128)(2,1)S(1)}, bf16[2048,256]{1,0:T(8,128)(2,1)}, u32[]{:S(2)}) copy-start(bf16[2048,256]{1,0:T(8,128)(2,1)} %w_h.1) | copy-start | bytes 3145732
  4.7 0.9 %copy-start.3 = (bf16[256,512]{1,0:T(8,128)(2,1)S(1)}, bf16[256,512]{1,0:T(8,128)(2,1)}, u32[]{:S(2)}) copy-start(bf16[256,512]{1,0:T(8,128)(2,1)} %ck_h.1) | copy-start | bytes 786436
  5.6 0.9 %copy-start.4 = (bf16[256,512]{1,0:T(8,128)(2,1)S(1)}, bf16[256,512]{1,0:T(8,128)(2,1)}, u32[]{:S(2)}) copy-start(bf16[256,512]{1,0:T(8,128)(2,1)} %cv_h.1) | copy-start | bytes 786436
  6.6 0.8 copy-start.5
  7.3 0.8 copy-start.6

commit v2 on v1

--- a/solution.py
+++ b/solution.py
@@ -17,7 +17,7 @@
 
 
 def kernel(dims, cq_h, ck_h, cv_h, qq_h, qk_h, qv_h, w_h, co_h, qo_h, cq, ck, cv, ak, av, qq, w, kb, vb, kqb, vqb,
-           acc, top, osend, lsend, orecv, lrecv, att, ysend, yrecv, co, qo, loc_sem, kv_s, kv_r, an_s, an_r, an_u,
+           acc, top, osend, lsend, orecv, lrecv, att, ysend, yrecv, co, qo, own_bias, query_bias, loc_sem, kv_s, kv_r, an_s, an_r, an_u,
            an_rs, an_rr, rs_s, rs_r, ag_r, ag_u, ag_d, ag_rs, ag_cs, y_s, y_r):
     groups, members, tps, kv_local, group, block, share, query_len = dims
     flat = group * query_len
@@ -105,6 +105,14 @@
         for copy in kv_copies(lax.rem(g + d, groups), g):
             copy.start()
 
+    at = lax.broadcasted_iota(jnp.int32, own_bias.shape, 0)
+    own_bias[...] = jnp.where(lax.broadcasted_iota(jnp.int32, own_bias.shape, 1) <= at, 0.0, NEG)
+    col = lax.broadcasted_iota(jnp.int32, (1, query_bias.shape[1]), 1)
+    position = (lax.div(col, share) * members + m) * share + lax.rem(col, share)
+    position = jnp.where(col < groups * share, position, query_len)
+    at = lax.broadcasted_iota(jnp.int32, query_bias.shape, 0)
+    query_bias[...] = jnp.where(at >= position, 0.0, NEG)
+
     def attend(first_row, first, slot, with_query):
         head = lax.div(first_row, query_len)
         row = lax.rem(first_row, query_len)
@@ -116,12 +124,8 @@
         values = jnp.concatenate([values, jnp.ones_like(values)], 1)
         s = lax.dot_general(q, keys, (((1,), (1,)), ((), ())), preferred_element_type=F32) * COEF
         if with_query:
-            col = lax.broadcasted_iota(jnp.int32, s.shape, 1) - block
-            at = lax.broadcasted_iota(jnp.int32, s.shape, 0) + row
-            source = lax.div(jnp.maximum(col, 0), share)
-            position = (source * members + m) * share + lax.rem(jnp.maximum(col, 0), share)
-            seen = (col < 0) | ((at >= position) & (col < groups * share))
-            s = jnp.where(seen, s, NEG)
+            bias = query_bias[pl.ds(pl.multiple_of(row, tile), tile), :]
+            s = jnp.concatenate([s[:, :block], s[:, block:] + bias], 1)
         rows = pl.ds(pl.multiple_of(first_row, tile), tile)
         high = jnp.max(s, axis=1, keepdims=True)
         if not first:
@@ -174,16 +178,7 @@
 
         lax.fori_loop(1, members, spread, 0)
 
-    @pl.when(not_root)
-    def _():
-        def gather(p, carry):
-            @pl.when(p != m)
-            def _():
-                for k, buf in enumerate((ak, av)):
-                    remote(buf.at[piece_rows(p)], buf.at[piece_rows(p)], an_u.at[k], an_rr.at[p, k], me).wait_recv()
-            return carry
-
-        lax.fori_loop(0, pieces, gather, 0)
+    anchor_bias = jnp.where(not_root, 0.0, NEG)
 
     def context_head(h):
         kv = lanes(lax.div(h, group))
@@ -192,20 +187,21 @@
         values = jnp.concatenate([av[:, kv], cv[:, kv]], 0)
         values = jnp.concatenate([values, jnp.ones_like(values)], 1)
         s = lax.dot_general(q, keys, (((1,), (1,)), ((), ())), preferred_element_type=F32) * COEF
-        col = lax.broadcasted_iota(jnp.int32, s.shape, 1) - block
-        at = lax.broadcasted_iota(jnp.int32, s.shape, 0)
-        s = jnp.where((col <= at) & ((col >= 0) | not_root), s, NEG)
+        s = jnp.concatenate([s[:, :block] + anchor_bias, s[:, block:] + own_bias[...]], 1)
         p = jnp.exp2(s - jnp.max(s, axis=1, keepdims=True)).astype(BF16)
         o = jnp.dot(p, values, preferred_element_type=F32)
         co[:, lanes(h)] = (o[:, :HD] / o[:, HD:]).astype(BF16)
 
-    def context_step(h, carry):
-        context_head(h)
-        return carry
-
-    lax.fori_loop(0, kv_local * group, context_step, 0, unroll=2)
-    store_ctx = local(co, co_h, 11)
-    store_ctx.start()
+    heads = kv_local * group
+
+    def context_heads(stage):
+        first, end = stage * heads // groups, (stage + 1) * heads // groups
+
+        def step(h, carry):
+            context_head(h)
+            return carry
+
+        lax.fori_loop(first, end, step, 0, unroll=2)
 
     for d in range(1, groups):
         slot = lax.rem(g + d, groups)
@@ -243,7 +239,19 @@
 
     lax.fori_loop(1, members, send_part, 0)
     attend_chunk(m)
-    own, own_lse = part(m)
+
+    @pl.when(not_root)
+    def _():
+        def gather(p, carry):
+            @pl.when(p != m)
+            def _():
+                for k, buf in enumerate((ak, av)):
+                    remote(buf.at[piece_rows(p)], buf.at[piece_rows(p)], an_u.at[k], an_rr.at[p, k], me).wait_recv()
+            return carry
+
+        lax.fori_loop(0, pieces, gather, 0)
+
+    context_heads(0)
 
     def wait_part(i, carry):
         for copy in part_copies(lax.rem(m + i, members), lax.rem(m + i, members)):
@@ -256,6 +264,7 @@
         row = lrecv[lax.rem(m + i, members)][:1, :]
         return jnp.transpose(jnp.broadcast_to(row, (HD, chunk)))
 
+    own, own_lse = part(m)
     highest = lax.fori_loop(1, members, lambda i, high: jnp.maximum(high, lse_of(i)), own_lse)
     own_weight = jnp.exp2(own_lse - highest)
 
@@ -326,6 +335,7 @@
     relay_down(0)
     have(g)
     for s in range(1, groups):
+        context_heads(s)
         when_low(s, arrive)
         relay_up(s)
         when_low(s, have)
@@ -343,6 +353,9 @@
         when_low(groups - 1, forward)
         when_high(groups - 1, forward)
 
+    store_ctx = local(co, co_h, 11)
+    store_ctx.start()
+
     def from_pair(i, carry):
         for c in range(groups):
             gathered(c, lax.rem(pair + 2 * i, members), ag_u.at[c], me).wait_recv()
@@ -456,7 +469,7 @@
     out_cols = out_weight.shape[1]
     out_rows = query_len // tps
     dims = (groups, members, tps, kv_local, group, block, share, query_len)
-    any_spec = pl.BlockSpec(memory_space=pl.ANY)
+    any_spec = pl.BlockSpec(memory_space=pltpu.HBM)
     dma = pltpu.SemaphoreType.DMA
     vmem = pltpu.VMEM
     return pl.pallas_call(
@@ -490,6 +503,8 @@
             vmem((tps, out_rows, out_cols), BF16),
             vmem((block, heads_wide), BF16),
             vmem((out_rows, out_cols), BF16),
+            vmem((block, block), F32),
+            vmem((query_len, query_rows), F32),
             dma((13,)),
             dma((groups, 4)),
             dma((groups, 4)),
@@ -509,7 +524,7 @@
             dma((tps,)),
         ],
         compiler_params=pltpu.CompilerParams(
-            collective_id=0, has_side_effects=True, vmem_limit_bytes=48 * 1024 * 1024
+            collective_id=0, has_side_effects=True, vmem_limit_bytes=64 * 1024 * 1024
         ),
         cost_estimate=pl.CostEstimate(flops=3_000_000_000, bytes_accessed=8_000_000, transcendentals=4_000_000),
         name="star_attention",

time: 88.5 us -> 70.4 us (0.80)
  Pallas kernels: 78.3 us -> 66.6 us
  local copies, waits for them, and re-layouts: 9.07 us -> 3 us
    pallas_call x1, Pallas kernels: 78.3 us -> 66.6 us  [body(): pl.pallas_call(functools.partial(kernel, dims), out_shape=(jax.ShapeDtype...]
    unnamed x16 -> x4, local copies, waits for them, and re-layouts: 9.07 us -> 3 us
where the time goes in v2:
time: 70.4 us; the launch traced here: 70.3 us
  Pallas kernels  66.6 us (95%)
  local copies, waits for them, and re-layouts  3 us (4%)
    pallas_call x1, Pallas kernels, body(): pl.pallas_call(functools.partial(kernel, dims), out_shape=(jax.ShapeDtype...  66.6 us
    unnamed x4, local copies, waits for them, and re-layouts  3 us

profile of v2, /device:TPU:0, one launch (start us, length us, event | category | flops | bytes accessed | tf_op | source)
XLA Modules:
  0.0 70.3 jit_solution(11442932327798251779)
XLA Ops:
  0.6 66.6 %star_attention.1 = (bf16[256,2048]{1,0:T(8,128)(2,1)}, bf16[256,256]{1,0:T(8,128)(2,1)}) custom-call(bf16[256,2048]{1,0:T(8,128)(2,1)} %cq_h.1, bf16[256,512]{1,0:T(8,128)(2,1)} %ck_h.1, bf16[256,512]{1,0:T(8,128)(2,1)} %cv_h.1, bf16[512,2048]{1,0:T(8,128)(2,1)} %qq_h.1, bf16[32,512]{1,0:T(8,128)(2,1)} %qk_h.1, bf16[32,512]{1,0:T(8,128)(2,1)} %qv_h.1, ...), custom_call_target="tpu_custom_call" | custom-call | flops 3000000000 | bytes 8000000 | tf_op jit(solution)/shard_map/star_attention/pallas_call | solution.py:475
  67.3 0.0 copy-start
  67.3 2.3 %copy.11 = bf16[256,2048]{1,0:T(8,128)(2,1)} copy(bf16[256,2048]{1,0:T(8,128)(2,1)} %get-tuple-element.4) | data formatting | bytes 2097152
  69.6 0.0 copy-done
  69.6 0.7 copy.12
Async XLA Ops:
  67.3 2.4 %copy-start = (bf16[256,256]{1,0:T(8,128)(2,1)S(1)}, bf16[256,256]{1,0:T(8,128)(2,1)}, u32[]{:S(2)}) copy-start(bf16[256,256]{1,0:T(8,128)(2,1)} %get-tuple-element.5) | copy-start | bytes 393220

commit v3 on v2

--- a/solution.py
+++ b/solution.py
@@ -228,7 +228,7 @@
         ]
 
     def send_part(i, carry):
-        to = lax.rem(m + i, members)
+        to = jnp.where(i < members - 1, lax.rem(m - lax.rem(m, 2) + 1 + i, members), pair)
         attend_chunk(to)
         out, lse = part(to)
         osend[to] = out.astype(BF16)
@@ -275,93 +275,124 @@
 
     total, summed = lax.fori_loop(1, members, combine, (own_weight, own_weight * own))
 
-    def place(of_group, of_member):
+    half = chunk // 2
+    mates = members // 2
+
+    def place(of_group, of_member, part_of):
         start = of_member * chunk
-        row = pl.multiple_of(lax.rem(start, query_len), chunk)
-        return att.at[pl.ds(row, chunk), lanes(of_group * group + lax.div(start, query_len))]
-
-    place(g, m)[...] = (summed / total).astype(BF16)
-
-    def gathered(of_group, of_member, send, to):
-        where = place(of_group, of_member)
-        return remote(where, where, send, ag_r.at[of_group, of_member], to)
-
-    def to_pair(of_group, of_member):
-        return gathered(of_group, of_member, ag_cs.at[of_group, of_member], g * members + pair)
-
-    def have(of_group):
-        def across(i, carry):
-            other = lax.rem(m + 2 * i, members)
-            gathered(of_group, m, ag_rs.at[of_group, other], g * members + other).start()
+        row = pl.multiple_of(lax.rem(start, query_len) + part_of * half, half)
+        return att.at[pl.ds(row, half), lanes(of_group * group + lax.div(start, query_len))]
+
+    attended = (summed / total).astype(BF16)
+    for h in range(2):
+        place(g, m, h)[...] = attended[h * half:(h + 1) * half]
+
+    def gathered(of_group, of_member, part_of, send, to):
+        where = place(of_group, of_member, part_of)
+        return remote(where, where, send, ag_r.at[of_group, of_member, part_of], to)
+
+    def mate(i):
+        return lax.rem(m + 2 * i, members)
+
+    def over_mates(first, run):
+        def step(i, carry):
+            run(mate(i))
             return carry
 
-        lax.fori_loop(1, members // 2, across, 0)
-        to_pair(of_group, m).start()
-
-    def forward(of_group):
-        def step(i, carry):
-            other = lax.rem(m + 2 * i, members)
-            gathered(of_group, other, ag_cs.at[of_group, other], me).wait_recv()
-            to_pair(of_group, other).start()
-            return carry
-
-        lax.fori_loop(1, members // 2, step, 0)
+        lax.fori_loop(first, mates, step, 0)
 
     up = lax.rem(me + members, groups * members)
     down = lax.rem(me + (groups - 1) * members, groups * members)
 
+    def to_pair(c, i, h):
+        return gathered(c, i, h, ag_cs.at[c, i, h], g * members + pair)
+
+    def across(c, h, other):
+        return gathered(c, m, h, ag_rs.at[c, other, h], g * members + other)
+
+    def go_up(c, i, h):
+        return gathered(c, i, h, ag_u.at[c, i, h], up)
+
+    def go_down(c, i, h):
+        return gathered(c, i, h, ag_d.at[c, i, h], down)
+
+    def arrive(c, i, h):
+        gathered(c, i, h, ag_cs.at[c, i, h], me).wait_recv()
+
+    def relay_up(c, i, h):
+        pl.when(g + 1 < groups)(lambda: go_up(c, i, h).start())
+
+    def relay_down(c, i, h):
+        pl.when(g > 0)(lambda: go_down(c, i, h).start())
+
     def when_low(s, run):
         pl.when(g - s >= 0)(lambda: run(jnp.maximum(g - s, 0)))
 
     def when_high(s, run):
         pl.when(g + s < groups)(lambda: run(jnp.minimum(g + s, groups - 1)))
 
-    def relay_up(s):
-        @pl.when((g - s >= 0) & (g + 1 < groups))
-        def _():
-            c = jnp.maximum(g - s, 0)
-            gathered(c, m, ag_u.at[c], up).start()
-
-    def relay_down(s):
-        @pl.when((g + s < groups) & (g > 0))
-        def _():
-            c = jnp.minimum(g + s, groups - 1)
-            gathered(c, m, ag_d.at[c], down).start()
-
-    def arrive(c):
-        gathered(c, m, ag_u.at[c], me).wait_recv()
-
-    relay_up(0)
-    relay_down(0)
-    have(g)
+    def from_column(relay):
+        def run(c):
+            arrive(c, m, 0)
+            relay(c, m, 0)
+            over_mates(1, lambda other: across(c, 0, other).start())
+            to_pair(c, m, 0).start()
+
+            def second(i):
+                arrive(c, i, 1)
+                relay(c, i, 1)
+                to_pair(c, i, 1).start()
+
+            over_mates(0, second)
+
+        return run
+
+    def from_row(c):
+        def first_half(i):
+            arrive(c, i, 0)
+            to_pair(c, i, 0).start()
+
+        over_mates(1, first_half)
+
+    over_mates(1, lambda other: across(g, 1, other).start())
+    for h in range(2):
+        relay_up(g, m, h)
+        relay_down(g, m, h)
+    over_mates(1, lambda other: across(g, 0, other).start())
+    for h in range(2):
+        to_pair(g, m, h).start()
+
+    def second_half(i):
+        arrive(g, i, 1)
+        relay_up(g, i, 1)
+        relay_down(g, i, 1)
+        to_pair(g, i, 1).start()
+
+    over_mates(1, second_half)
     for s in range(1, groups):
         context_heads(s)
-        when_low(s, arrive)
-        relay_up(s)
-        when_low(s, have)
-        when_high(s, arrive)
-        relay_down(s)
-        when_high(s, have)
+        when_low(s, from_column(relay_up))
+        when_high(s, from_column(relay_down))
         if s == 1:
-            forward(g)
+            from_row(g)
         else:
-            when_low(s - 1, forward)
-            when_high(s - 1, forward)
+            when_low(s - 1, from_row)
+            when_high(s - 1, from_row)
     if groups == 1:
-        forward(g)
+        from_row(g)
     else:
-        when_low(groups - 1, forward)
-        when_high(groups - 1, forward)
-
+        when_low(groups - 1, from_row)
+        when_high(groups - 1, from_row)
     store_ctx = local(co, co_h, 11)
     store_ctx.start()
 
     def from_pair(i, carry):
         for c in range(groups):
-            gathered(c, lax.rem(pair + 2 * i, members), ag_u.at[c], me).wait_recv()
+            for h in range(2):
+                arrive(c, lax.rem(pair + 2 * i, members), h)
         return carry
 
-    lax.fori_loop(0, members // 2, from_pair, 0)
+    lax.fori_loop(0, mates, from_pair, 0)
 
     out_rows = query_len // tps
 
@@ -421,32 +452,20 @@
         return carry
 
     lax.fori_loop(1, members, part_done, 0)
-    for s in range(groups):
-        @pl.when((g - s >= 0) & (g + 1 < groups))
+
+    def column_done(c, towards, can):
+        @pl.when(can)
         def _():
-            c = jnp.maximum(g - s, 0)
-            gathered(c, m, ag_u.at[c], up).wait_send()
-
-        @pl.when((g + s < groups) & (g > 0))
-        def _():
-            c = jnp.minimum(g + s, groups - 1)
-            gathered(c, m, ag_d.at[c], down).wait_send()
-
-    def pair_done(i, carry):
-        other = lax.rem(m + 2 * i, members)
-        for c in range(groups):
-            to_pair(c, other).wait_send()
-        return carry
-
-    lax.fori_loop(0, members // 2, pair_done, 0)
-
-    def across_done(i, carry):
-        other = lax.rem(m + 2 * i, members)
-        for c in range(groups):
-            gathered(c, m, ag_rs.at[c, other], me).wait_send()
-        return carry
-
-    lax.fori_loop(1, members // 2, across_done, 0)
+            towards(c, m, 0).wait_send()
+            over_mates(0, lambda i: towards(c, i, 1).wait_send())
+
+    for c in range(groups):
+        column_done(c, go_up, (c <= g) & (g + 1 < groups))
+        column_done(c, go_down, (c >= g) & (g > 0))
+        for h in range(2):
+            over_mates(0, lambda i: to_pair(c, i, h).wait_send())
+        over_mates(1, lambda other: across(c, 0, other).wait_send())
+    over_mates(1, lambda other: across(g, 1, other).wait_send())
     for d in range(1, tps):
         sum_copy(lax.rem(my_tp + d, tps), my_tp).wait_send()
     store_ctx.wait()
@@ -515,11 +534,11 @@
             dma((pieces, 2)),
             dma((members, 2)),
             dma((members, 2)),
-            dma((groups, members)),
-            dma((groups,)),
-            dma((groups,)),
-            dma((groups, members)),
-            dma((groups, members)),
+            dma((groups, members, 2)),
+            dma((groups, members, 2)),
+            dma((groups, members, 2)),
+            dma((groups, members, 2)),
+            dma((groups, members, 2)),
             dma((tps,)),
             dma((tps,)),
         ],

time: 70.4 us -> 66.7 us (0.947)
  Pallas kernels: 66.6 us -> 62.9 us
    pallas_call x1, Pallas kernels: 66.6 us -> 62.9 us  [body(): pl.pallas_call(functools.partial(kernel, dims), out_shape=(jax.ShapeDtype...]
where the time goes in v3:
time: 66.7 us; the launch traced here: 66.5 us
  Pallas kernels  62.9 us (94%)
  local copies, waits for them, and re-layouts  3 us (4%)
    pallas_call x1, Pallas kernels, body(): pl.pallas_call(functools.partial(kernel, dims), out_shape=(jax.ShapeDtype...  62.9 us
    unnamed x4, local copies, waits for them, and re-layouts  3 us

profile of v3, /device:TPU:0, one launch (start us, length us, event | category | flops | bytes accessed | tf_op | source)
XLA Modules:
  0.0 66.5 jit_solution(2275705856626688444)
XLA Ops:
  0.6 62.9 %star_attention.1 = (bf16[256,2048]{1,0:T(8,128)(2,1)}, bf16[256,256]{1,0:T(8,128)(2,1)}) custom-call(bf16[256,2048]{1,0:T(8,128)(2,1)} %cq_h.1, bf16[256,512]{1,0:T(8,128)(2,1)} %ck_h.1, bf16[256,512]{1,0:T(8,128)(2,1)} %cv_h.1, bf16[512,2048]{1,0:T(8,128)(2,1)} %qq_h.1, bf16[32,512]{1,0:T(8,128)(2,1)} %qk_h.1, bf16[32,512]{1,0:T(8,128)(2,1)} %qv_h.1, ...), custom_call_target="tpu_custom_call" | custom-call | flops 3000000000 | bytes 8000000 | tf_op jit(solution)/shard_map/star_attention/pallas_call | solution.py:494
  63.5 0.0 copy-start
  63.5 2.3 %copy.11 = bf16[256,2048]{1,0:T(8,128)(2,1)} copy(bf16[256,2048]{1,0:T(8,128)(2,1)} %get-tuple-element.4) | data formatting | bytes 2097152
  65.9 0.0 copy-done
  65.9 0.7 copy.12
Async XLA Ops:
  63.5 2.4 %copy-start = (bf16[256,256]{1,0:T(8,128)(2,1)S(1)}, bf16[256,256]{1,0:T(8,128)(2,1)}, u32[]{:S(2)}) copy-start(bf16[256,256]{1,0:T(8,128)(2,1)} %get-tuple-element.5) | copy-start | bytes 393220

commit v4 on v3

--- a/solution.py
+++ b/solution.py
@@ -101,8 +101,20 @@
             remote(qv_h.at[:, lanes(to_group)], vqb.at[rows], kv_s.at[to_group, 3], kv_r.at[slot, 3], to),
         ]
 
+    def other_group(d):
+        if groups & (groups - 1):
+            return lax.rem(g + d, groups)
+        other = g
+        for bit in range(groups.bit_length()):
+            if d >> bit & 1:
+                other = other + (1 << bit) * (1 - 2 * lax.rem(lax.div(g, 1 << bit), 2))
+        return other
+
     for d in range(1, groups):
-        for copy in kv_copies(lax.rem(g + d, groups), g):
+        for copy in kv_copies(other_group(d), g)[2:]:
+            copy.start()
+    for d in range(1, groups):
+        for copy in kv_copies(other_group(d), g)[:2]:
             copy.start()
 
     at = lax.broadcasted_iota(jnp.int32, own_bias.shape, 0)
@@ -138,9 +150,9 @@
         acc[rows, :] = o
         top[rows, :] = jnp.broadcast_to(high, (tile, HD))
 
-    def sweep(slot, first):
+    def sweep(slot, first, with_query):
         def step(t, carry):
-            attend(t * tile, first, slot, False)
+            attend(t * tile, first, slot, with_query)
             return carry
 
         lax.fori_loop(0, flat // tile, step, 0, unroll=2)
@@ -148,7 +160,7 @@
     for i in (0, 1, 2):
         loads[i].wait()
     if groups > 1:
-        sweep(g, True)
+        sweep(g, True, False)
 
     for i in (3, 4, 5, 6, 7, 8):
         loads[i].wait()
@@ -204,12 +216,16 @@
         lax.fori_loop(first, end, step, 0, unroll=2)
 
     for d in range(1, groups):
-        slot = lax.rem(g + d, groups)
-        for copy in kv_copies(slot, slot):
+        slot = other_group(d)
+        if d == 1:
+            for e in range(1, groups):
+                for copy in kv_copies(other_group(e), other_group(e))[2:]:
+                    copy.wait_recv()
+        for copy in kv_copies(slot, slot)[:2]:
             copy.wait_recv()
         if d < groups - 1:
-            sweep(slot, False)
-    last = lax.rem(g + groups - 1, groups)
+            sweep(slot, False, d == 1)
+    last = other_group(groups - 1)
 
     def part(to):
         rows = pl.ds(pl.multiple_of(to * chunk, chunk), chunk)
@@ -218,7 +234,7 @@
 
     def attend_chunk(to):
         for t in range(chunk // tile):
-            attend(to * chunk + t * tile, groups == 1, last, True)
+            attend(to * chunk + t * tile, groups == 1, last, groups <= 2)
 
     def part_copies(to, slot):
         target = g * members + to
@@ -494,11 +510,11 @@
     return pl.pallas_call(
         functools.partial(kernel, dims),
         out_shape=(
-            jax.ShapeDtypeStruct((block, heads_wide), BF16),
-            jax.ShapeDtypeStruct((out_rows, out_cols), BF16),
+            pltpu.VMEM((block, heads_wide), BF16),
+            pltpu.VMEM((out_rows, out_cols), BF16),
         ),
         in_specs=[any_spec] * 7,
-        out_specs=(any_spec, any_spec),
+        out_specs=(pl.BlockSpec(memory_space=pl.ANY),) * 2,
         scratch_shapes=[
             vmem((block, heads_wide), BF16),
             vmem((block, kv_wide), BF16),
@@ -543,7 +559,7 @@
             dma((tps,)),
         ],
         compiler_params=pltpu.CompilerParams(
-            collective_id=0, has_side_effects=True, vmem_limit_bytes=64 * 1024 * 1024
+            collective_id=0, has_side_effects=True, vmem_limit_bytes=62 * 1024 * 1024
         ),
         cost_estimate=pl.CostEstimate(flops=3_000_000_000, bytes_accessed=8_000_000, transcendentals=4_000_000),
         name="star_attention",

time: 66.7 us -> 65.8 us (0.987)
  local copies, waits for them, and re-layouts: 3 us -> 1.63 us
    unnamed x4 -> x2, local copies, waits for them, and re-layouts: 3 us -> 1.63 us
where the time goes in v4:
time: 65.8 us; the launch traced here: 65.6 us
  Pallas kernels  63.4 us (96%)
  local copies, waits for them, and re-layouts  1.63 us (2%)
    pallas_call x1, Pallas kernels, body(): pl.pallas_call(functools.partial(kernel, dims), out_shape=(pltpu.VMEM((bl...  63.4 us
    unnamed x2, local copies, waits for them, and re-layouts  1.63 us

profile of v4, /device:TPU:0, one launch (start us, length us, event | category | flops | bytes accessed | tf_op | source)
XLA Modules:
  0.0 65.6 jit_solution(869621997464153212)
XLA Ops:
  0.6 63.4 %star_attention.1 = (bf16[256,2048]{1,0:T(8,128)(2,1)S(1)}, bf16[256,256]{1,0:T(8,128)(2,1)S(1)}) custom-call(bf16[256,2048]{1,0:T(8,128)(2,1)} %cq_h.1, bf16[256,512]{1,0:T(8,128)(2,1)} %ck_h.1, bf16[256,512]{1,0:T(8,128)(2,1)} %cv_h.1, bf16[512,2048]{1,0:T(8,128)(2,1)} %qq_h.1, bf16[32,512]{1,0:T(8,128)(2,1)} %qk_h.1, bf16[32,512]{1,0:T(8,128)(2,1)} %qv_h.1, ...), custom_call_target="tpu_custom_call" | custom-call | flops 3000000000 | bytes 8000000 | tf_op jit(solution)/shard_map/star_attention/pallas_call | solution.py:510
  64.0 1.0 %copy.11 = bf16[256,2048]{1,0:T(8,128)(2,1)} copy(bf16[256,2048]{1,0:T(8,128)(2,1)S(1)} %get-tuple-element.2) | data formatting | bytes 2097152
  65.0 0.7 copy.12

commit v5 on v4

--- a/solution.py
+++ b/solution.py
@@ -57,8 +57,8 @@
     if kqb.shape[0] > groups * share:
         kqb[...] = jnp.zeros_like(kqb)
         vqb[...] = jnp.zeros_like(vqb)
-    for load in loads:
-        load.start()
+    for i in (3, 4, 0, 1, 2, 7, 8, 5, 6):
+        loads[i].start()
 
     @pl.when(me == 0)
     def _():
@@ -91,12 +91,15 @@
             for k, buf in enumerate((ak, av)):
                 remote(buf.at[piece_rows(p)], buf.at[piece_rows(p)], an_s.at[p, k], an_r.at[k], p).start()
 
+    loads[3].wait()
+    loads[4].wait()
+
     def kv_copies(to_group, slot):
         to = to_group * members + m
         rows = pl.ds(pl.multiple_of(slot * share, share), share)
         return [
-            remote(ck_h.at[:, lanes(to_group)], kb.at[slot], kv_s.at[to_group, 0], kv_r.at[slot, 0], to),
-            remote(cv_h.at[:, lanes(to_group)], vb.at[slot], kv_s.at[to_group, 1], kv_r.at[slot, 1], to),
+            remote(ck.at[:, lanes(to_group)], kb.at[slot], kv_s.at[to_group, 0], kv_r.at[slot, 0], to),
+            remote(cv.at[:, lanes(to_group)], vb.at[slot], kv_s.at[to_group, 1], kv_r.at[slot, 1], to),
             remote(qk_h.at[:, lanes(to_group)], kqb.at[rows], kv_s.at[to_group, 2], kv_r.at[slot, 2], to),
             remote(qv_h.at[:, lanes(to_group)], vqb.at[rows], kv_s.at[to_group, 3], kv_r.at[slot, 3], to),
         ]
@@ -162,7 +165,7 @@
     if groups > 1:
         sweep(g, True, False)
 
-    for i in (3, 4, 5, 6, 7, 8):
+    for i in (5, 6, 7, 8):
         loads[i].wait()
     not_root = me > 0
     has_piece = m < pieces
@@ -281,15 +284,24 @@
         return jnp.transpose(jnp.broadcast_to(row, (HD, chunk)))
 
     own, own_lse = part(m)
-    highest = lax.fori_loop(1, members, lambda i, high: jnp.maximum(high, lse_of(i)), own_lse)
-    own_weight = jnp.exp2(own_lse - highest)
-
-    def combine(i, carry):
-        total, summed = carry
-        weight = jnp.exp2(lse_of(i) - highest)
-        return total + weight, summed + weight * orecv[lax.rem(m + i, members)].astype(F32)
-
-    total, summed = lax.fori_loop(1, members, combine, (own_weight, own_weight * own))
+    if members <= 8:
+        lses = [own_lse] + [lse_of(i) for i in range(1, members)]
+        highest = functools.reduce(jnp.maximum, lses)
+        weights = [jnp.exp2(lse - highest) for lse in lses]
+        total = sum(weights)
+        summed = weights[0] * own
+        for i in range(1, members):
+            summed = summed + weights[i] * orecv[lax.rem(m + i, members)].astype(F32)
+    else:
+        highest = lax.fori_loop(1, members, lambda i, high: jnp.maximum(high, lse_of(i)), own_lse)
+        own_weight = jnp.exp2(own_lse - highest)
+
+        def combine(i, carry):
+            total, summed = carry
+            weight = jnp.exp2(lse_of(i) - highest)
+            return total + weight, summed + weight * orecv[lax.rem(m + i, members)].astype(F32)
+
+        total, summed = lax.fori_loop(1, members, combine, (own_weight, own_weight * own))
 
     half = chunk // 2
     mates = members // 2

time: 65.8 us -> 65.1 us (0.989)
  Pallas kernels: 63.4 us -> 62.7 us
    pallas_call x1, Pallas kernels: 63.4 us -> 62.7 us  [body(): pl.pallas_call(functools.partial(kernel, dims), out_shape=(pltpu.VMEM((bl...]
where the time goes in v5:
time: 65.1 us; the launch traced here: 65 us
  Pallas kernels  62.7 us (96%)
  local copies, waits for them, and re-layouts  1.63 us (3%)
    pallas_call x1, Pallas kernels, body(): pl.pallas_call(functools.partial(kernel, dims), out_shape=(pltpu.VMEM((bl...  62.7 us
    unnamed x2, local copies, waits for them, and re-layouts  1.63 us

profile of v5, /device:TPU:0, one launch (start us, length us, event | category | flops | bytes accessed | tf_op | source)
XLA Modules:
  0.0 65.0 jit_solution(10710721719101774797)
XLA Ops:
  0.6 62.7 %star_attention.1 = (bf16[256,2048]{1,0:T(8,128)(2,1)S(1)}, bf16[256,256]{1,0:T(8,128)(2,1)S(1)}) custom-call(bf16[256,2048]{1,0:T(8,128)(2,1)} %cq_h.1, bf16[256,512]{1,0:T(8,128)(2,1)} %ck_h.1, bf16[256,512]{1,0:T(8,128)(2,1)} %cv_h.1, bf16[512,2048]{1,0:T(8,128)(2,1)} %qq_h.1, bf16[32,512]{1,0:T(8,128)(2,1)} %qk_h.1, bf16[32,512]{1,0:T(8,128)(2,1)} %qv_h.1, ...), custom_call_target="tpu_custom_call" | custom-call | flops 3000000000 | bytes 8000000 | tf_op jit(solution)/shard_map/star_attention/pallas_call | solution.py:522
  63.4 1.0 %copy.11 = bf16[256,2048]{1,0:T(8,128)(2,1)} copy(bf16[256,2048]{1,0:T(8,128)(2,1)S(1)} %get-tuple-element.2) | data formatting | bytes 2097152
  64.3 0.7 %copy.12 = bf16[256,256]{1,0:T(8,128)(2,1)} copy(bf16[256,256]{1,0:T(8,128)(2,1)S(1)} %get-tuple-element.3) | data formatting | bytes 262144

commit v6 on v5

--- a/solution.py
+++ b/solution.py
@@ -210,7 +210,10 @@
     heads = kv_local * group
 
     def context_heads(stage):
-        first, end = stage * heads // groups, (stage + 1) * heads // groups
+        stages = max(groups - 1, 1)
+        first, end = [min(i, stages) * heads // stages for i in (stage, stage + 1)]
+        if first == end:
+            return
 
         def step(h, carry):
             context_head(h)

time: 65.1 us -> 66 us (1.014)
  Pallas kernels: 62.7 us -> 63.6 us
    pallas_call x1, Pallas kernels: 62.7 us -> 63.6 us  [body(): pl.pallas_call(functools.partial(kernel, dims), out_shape=(pltpu.VMEM((bl...]
where the time goes in v6:
time: 66 us; the launch traced here: 65.8 us
  Pallas kernels  63.6 us (96%)
  local copies, waits for them, and re-layouts  1.63 us (2%)
    pallas_call x1, Pallas kernels, body(): pl.pallas_call(functools.partial(kernel, dims), out_shape=(pltpu.VMEM((bl...  63.6 us
    unnamed x2, local copies, waits for them, and re-layouts  1.63 us

profile of v6, /device:TPU:0, one launch (start us, length us, event | category | flops | bytes accessed | tf_op | source)
XLA Modules:
  0.0 65.8 jit_solution(3354746531036118823)
XLA Ops:
  0.6 63.6 %star_attention.1 = (bf16[256,2048]{1,0:T(8,128)(2,1)S(1)}, bf16[256,256]{1,0:T(8,128)(2,1)S(1)}) custom-call(bf16[256,2048]{1,0:T(8,128)(2,1)} %cq_h.1, bf16[256,512]{1,0:T(8,128)(2,1)} %ck_h.1, bf16[256,512]{1,0:T(8,128)(2,1)} %cv_h.1, bf16[512,2048]{1,0:T(8,128)(2,1)} %qq_h.1, bf16[32,512]{1,0:T(8,128)(2,1)} %qk_h.1, bf16[32,512]{1,0:T(8,128)(2,1)} %qv_h.1, ...), custom_call_target="tpu_custom_call" | custom-call | flops 3000000000 | bytes 8000000 | tf_op jit(solution)/shard_map/star_attention/pallas_call | solution.py:525
  64.2 1.0 %copy.11 = bf16[256,2048]{1,0:T(8,128)(2,1)} copy(bf16[256,2048]{1,0:T(8,128)(2,1)S(1)} %get-tuple-element.2) | data formatting | bytes 2097152
  65.2 0.7 copy.12
